TPU v7x, 32 devices: a whole 2x2x4 slice. The times are simulated.
32 devices in a mesh: groups: 2 (over y), row: 4 (over z), col: 2 (over x), segment: 2 (over core).
Axes of the slice: x: 2, y: 2, z: 4, core: 2. Of those that a mesh axis runs over, the one named last changes fastest.
Arguments:
- latents: bfloat16 [4, 512, 3072], P(None, ('groups', 'col'), 'row'), parts along dimension 1, may hold values from -6 to 6
- w_in: bfloat16 [2, 3072, 12288], P('segment', 'col', 'row'), may hold values from -0.109375 to 0.109375
- b_in: float32 [2, 12288], P('segment', 'row'), may hold values from -4 to 4
- w_out: bfloat16 [2, 12288, 3072], P('segment', 'row', 'col'), may hold values from -0.0546875 to 0.0546875
- b_out: float32 [2, 3072], P('segment', 'row'), may hold values from -3 to 3
- modulation: float32 [2, 8, 3, 3072], P('segment', 'groups'), parts along dimension 1, may hold values from -3 to 3
Outputs:
- layer_outputs: bfloat16 [2, 4, 512, 3072], P('segment', None, ('groups', 'col'), 'row'), parts along dimension 2
There are 2 independent parts, one for each index of `groups`. A program takes and returns all parts, laid end to end along the dimension named above; an argument that names none is the same for every part. Nothing has to cross between parts.
All inputs are finite; a program needn't handle non-finite values.
Results may differ from a plain program's by a relative error of at most 0.009.
Values may be sent and summed in bfloat16 or wider, within the bound.
A program may use at most 128 MiB of HBM per device.

v0:
```python
import jax
import jax.numpy as jnp
from jax import lax
from jax.sharding import PartitionSpec as P


def shifted(block, axis, distance):
    devices = range(lax.axis_size(axis))
    route = [(i - distance, i) for i in devices if i - distance in devices]
    return lax.ppermute(block, axis, route)


def on_device(latents, w_in, b_in, w_out, b_out, modulation):
    panels = (
        lax.all_gather(w_in, "col", axis=1, tiled=True),
        lax.all_gather(w_out, "col", axis=2, tiled=True),
    )
    w_first = panels[0][0]
    w_second = panels[1][0]
    micro_count = latents.shape[0]
    width = latents.shape[2]
    segment = lax.axis_index("segment")
    segments = lax.axis_size("segment")
    ticks = micro_count + segments - 1
    row_start = lax.axis_index("row") * width
    conditioning = modulation[0]
    bias_first = b_in[0]
    bias_local = b_out[0]
    results = []
    handed = jnp.zeros_like(latents[0])
    for tick in range(ticks):
        if tick > 0:
            handed = shifted(results[-1], "segment", 1)
        first_feed = latents[min(tick, micro_count - 1)]
        feed = jnp.where(segment == 0, first_feed, handed)
        micro = jnp.clip(tick - segment, 0, micro_count - 1)
        mods = lax.dynamic_index_in_dim(conditioning, micro, 0, keepdims=False)
        values = feed.astype(jnp.float32)
        whole = lax.all_gather(feed, "row", axis=1, tiled=True).astype(jnp.float32)
        mean = jnp.mean(whole, axis=-1, keepdims=True)
        var = jnp.mean((whole - mean) ** 2, axis=-1, keepdims=True)
        normed = (whole - mean) * lax.rsqrt(var + 1e-06)
        modulated = (normed * (1.0 + mods[1]) + mods[0]).astype(jnp.bfloat16)
        pre = jnp.dot(modulated, w_first, preferred_element_type=jnp.float32)
        hidden = jax.nn.gelu(pre + bias_first, approximate=True).astype(jnp.bfloat16)
        term = jnp.dot(hidden, w_second, preferred_element_type=jnp.float32)
        branch = lax.psum_scatter(
            term.astype(jnp.bfloat16), "row", scatter_dimension=1, tiled=True
        ).astype(jnp.float32)
        gate_local = lax.dynamic_slice_in_dim(mods[2], row_start, width, 0)
        results.append((values + gate_local * (branch + bias_local)).astype(jnp.bfloat16))
    stacked = jnp.stack(results)
    chosen = lax.dynamic_slice_in_dim(stacked, segment, micro_count, 0)
    return chosen[None]


def solution(mesh):
    return jax.shard_map(
        on_device,
        mesh=mesh,
        in_specs=(
            P(None, ("groups", "col"), "row"),
            P("segment", "col", "row"),
            P("segment", "row"),
            P("segment", "row", "col"),
            P("segment", "row"),
            P("segment", "groups", None, None),
        ),
        out_specs=P("segment", None, ("groups", "col"), "row"),
        check_vma=False,
    )
```

profile of v0, /device:TPU:15, one launch (start us, length us, event | category | flops | bytes accessed | tf_op | source)
XLA Modules:
  0.0 764.1 jit_solution(15648472256520840852)
XLA Ops:
  6.5 0.7 all-gather.4.cloned.1.call-update
  8.4 16.3 %all-gather = bf16[1,128,3072]{2,1,0:T(8,128)(2,1)S(1)} all-gather(bf16[1,128,768]{2,1,0:T(8,128)(2,1)S(1)} %slice_select_fusion), channel_id=2, replica_groups=mesh['groups'=2,'row'=4,'col'=2,'segment'=2] {'row'}, dimensions={2}, use_global_device_ids=true | all-gather | bytes 983040 | tf_op jit(solution)/shard_map/all_gather | solution.py:39
  25.5 208.0 %all-gather.4.cloned.1.call-done = bf16[1,3072,3072]{2,1,0:T(8,128)(2,1)} async-done(((bf16[1,1536,3072]{2,1,0:T(8,128)(2,1)}), bf16[1,3072,3072]{2,1,0:T(8,128)(2,1)}) %all-gather.4.cloned.1.call-update) | async-done | bytes 18874384 | tf_op jit(solution)/shard_map/all_gather | solution.py:15
  233.5 225.9 %all-gather.6.cloned.1.call-done = bf16[1,3072,3072]{2,1,0:T(8,128)(2,1)} async-done(((bf16[1,3072,1536]{2,1,0:T(8,128)(2,1)}), bf16[1,3072,3072]{2,1,0:T(8,128)(2,1)}) %all-gather.6.cloned.1.call-update) | async-done | bytes 18874384 | tf_op jit(solution)/shard_map/all_gather | solution.py:16
  459.4 18.4 %fusion.35 = bf16[128,3072]{1,0:T(8,128)(2,1)} fusion(bf16[1,3072,3072]{2,1,0:T(8,128)(2,1)} %all-gather.6.cloned.1.call-done, bf16[1,3072,3072]{2,1,0:T(8,128)(2,1)} %all-gather.4.cloned.1.call-done, bf16[1,128,3072]{2,1,0:T(8,128)(2,1)S(1)} %all-gather, f32[3072]{0:T(1024)S(1)} %bitcast.137, f32[3072]{0:T(1024)S(1)} %bitcast.136, f32[3072]{0:T(1024)S(1)} %bitcast.135, ...), kind=kOutput, calls=%fused_computation.25 | convolution fusion | flops 4838522880 | bytes 39359488 | tf_op jit(solution)/shard_map/dot_general | solution.py:46
  478.1 22.0 %reduce-scatter.6.cloned.1.call-done = bf16[128,768]{1,0:T(8,128)(2,1)} async-done(((bf16[128,3072]{1,0:T(8,128)(2,1)}), bf16[128,768]{1,0:T(8,128)(2,1)}) %reduce-scatter.6.cloned.1.call-update) | async-done | bytes 196624 | tf_op jit(solution)/shard_map/reduce_scatter | solution.py:47
  500.1 1.0 bitcast_dynamic-update-slice_fusion.3
  501.1 1.3 collective-permute-start
  502.4 2.0 collective-permute-done
  504.5 16.9 %all_gather.24 = bf16[128,3072]{1,0:T(8,128)(2,1)S(1)} all-gather(bf16[128,768]{1,0:T(8,128)(2,1)S(1)} %bitcast_select_fusion.3), channel_id=1, replica_groups=mesh['groups'=2,'row'=4,'col'=2,'segment'=2] {'row'}, dimensions={1}, use_global_device_ids=true | all-gather | bytes 983040 | tf_op jit(solution)/shard_map/all_gather | solution.py:39
  521.9 18.4 %fusion.38 = bf16[128,3072]{1,0:T(8,128)(2,1)} fusion(bf16[1,3072,3072]{2,1,0:T(8,128)(2,1)} %all-gather.6.cloned.1.call-done, bf16[1,3072,3072]{2,1,0:T(8,128)(2,1)} %all-gather.4.cloned.1.call-done, bf16[128,3072]{1,0:T(8,128)(2,1)S(1)} %all_gather.24, f32[3072]{0:T(1024)S(1)} %bitcast.134, f32[3072]{0:T(1024)S(1)} %bitcast.133, ...), kind=kOutput, calls=%fused_computation.26 | convolution fusion | flops 4838522880 | bytes 39359488 | tf_op jit(solution)/shard_map/dot_general | solution.py:46
  540.4 23.4 %reduce-scatter.8.cloned.1.call-done = bf16[128,768]{1,0:T(8,128)(2,1)} async-done(((bf16[128,3072]{1,0:T(8,128)(2,1)}), bf16[128,768]{1,0:T(8,128)(2,1)}) %reduce-scatter.8.cloned.1.call-update) | async-done | bytes 196624 | tf_op jit(solution)/shard_map/reduce_scatter | solution.py:47
  563.8 1.0 bitcast_dynamic-update-slice_fusion.2
  564.8 1.3 collective-permute-start.1
  566.1 2.0 collective-permute-done.1
  568.2 16.9 %all_gather.25 = bf16[128,3072]{1,0:T(8,128)(2,1)S(1)} all-gather(bf16[128,768]{1,0:T(8,128)(2,1)S(1)} %bitcast_select_fusion.2), channel_id=1, replica_groups=mesh['groups'=2,'row'=4,'col'=2,'segment'=2] {'row'}, dimensions={1}, use_global_device_ids=true | all-gather | bytes 983040 | tf_op jit(solution)/shard_map/all_gather | solution.py:39
  585.7 18.4 %fusion.41 = bf16[128,3072]{1,0:T(8,128)(2,1)} fusion(bf16[1,3072,3072]{2,1,0:T(8,128)(2,1)} %all-gather.6.cloned.1.call-done, bf16[1,3072,3072]{2,1,0:T(8,128)(2,1)} %all-gather.4.cloned.1.call-done, bf16[128,3072]{1,0:T(8,128)(2,1)S(1)} %all_gather.25, f32[3072]{0:T(1024)S(1)} %bitcast.132, f32[3072]{0:T(1024)S(1)} %bitcast.131, ...), kind=kOutput, calls=%fused_computation.27 | convolution fusion | flops 4838522880 | bytes 39359488 | tf_op jit(solution)/shard_map/dot_general | solution.py:46
  604.2 23.4 %reduce-scatter.10.cloned.1.call-done = bf16[128,768]{1,0:T(8,128)(2,1)} async-done(((bf16[128,3072]{1,0:T(8,128)(2,1)}), bf16[128,768]{1,0:T(8,128)(2,1)}) %reduce-scatter.10.cloned.1.call-update) | async-done | bytes 196624 | tf_op jit(solution)/shard_map/reduce_scatter | solution.py:47
  627.6 1.0 bitcast_dynamic-update-slice_fusion.1
  628.6 1.3 collective-permute-start.2
  629.9 2.0 collective-permute-done.2
  632.0 17.0 %all_gather.26 = bf16[128,3072]{1,0:T(8,128)(2,1)S(1)} all-gather(bf16[128,768]{1,0:T(8,128)(2,1)S(1)} %bitcast_select_fusion.1), channel_id=1, replica_groups=mesh['groups'=2,'row'=4,'col'=2,'segment'=2] {'row'}, dimensions={1}, use_global_device_ids=true | all-gather | bytes 983040 | tf_op jit(solution)/shard_map/all_gather | solution.py:39
  649.6 18.4 %fusion.44 = bf16[128,3072]{1,0:T(8,128)(2,1)} fusion(bf16[1,3072,3072]{2,1,0:T(8,128)(2,1)} %all-gather.6.cloned.1.call-done, bf16[1,3072,3072]{2,1,0:T(8,128)(2,1)} %all-gather.4.cloned.1.call-done, bf16[128,3072]{1,0:T(8,128)(2,1)S(1)} %all_gather.26, f32[3072]{0:T(1024)S(1)} %bitcast.130, f32[3072]{0:T(1024)S(1)} %bitcast.129, ...), kind=kOutput, calls=%fused_computation.28 | convolution fusion | flops 4838522880 | bytes 39359488 | tf_op jit(solution)/shard_map/dot_general | solution.py:46
  668.1 23.4 %reduce-scatter.12.cloned.1.call-done = bf16[128,768]{1,0:T(8,128)(2,1)} async-done(((bf16[128,3072]{1,0:T(8,128)(2,1)}), bf16[128,768]{1,0:T(8,128)(2,1)}) %reduce-scatter.12.cloned.1.call-update) | async-done | bytes 196624 | tf_op jit(solution)/shard_map/reduce_scatter | solution.py:47
  691.5 1.0 bitcast_dynamic-update-slice_fusion
  692.5 1.3 collective-permute-start.3
  693.8 2.0 collective-permute-done.3
  695.9 17.1 %all_gather.27 = bf16[128,3072]{1,0:T(8,128)(2,1)S(1)} all-gather(bf16[128,768]{1,0:T(8,128)(2,1)S(1)} %bitcast_select_fusion), channel_id=1, replica_groups=mesh['groups'=2,'row'=4,'col'=2,'segment'=2] {'row'}, dimensions={1}, use_global_device_ids=true | all-gather | bytes 983040 | tf_op jit(solution)/shard_map/all_gather | solution.py:39
  713.5 18.4 %fusion.47 = bf16[128,3072]{1,0:T(8,128)(2,1)} fusion(bf16[1,3072,3072]{2,1,0:T(8,128)(2,1)} %all-gather.6.cloned.1.call-done, bf16[1,3072,3072]{2,1,0:T(8,128)(2,1)} %all-gather.4.cloned.1.call-done, bf16[128,3072]{1,0:T(8,128)(2,1)S(1)} %all_gather.27, f32[3072]{0:T(1024)S(1)} %bitcast.128, f32[3072]{0:T(1024)S(1)} %bitcast.127, ...), kind=kOutput, calls=%fused_computation.29 | convolution fusion | flops 4838522880 | bytes 39359488 | tf_op jit(solution)/shard_map/dot_general | solution.py:46
  731.9 23.4 %reduce-scatter.14.cloned.1.call-done = bf16[128,768]{1,0:T(8,128)(2,1)} async-done(((bf16[128,3072]{1,0:T(8,128)(2,1)}), bf16[128,768]{1,0:T(8,128)(2,1)}) %reduce-scatter.14.cloned.1.call-update) | async-done | bytes 196624 | tf_op jit(solution)/shard_map/reduce_scatter | solution.py:47
  755.3 1.0 fusion.188
  756.3 0.9 dynamic-slice_bitcast_fusion
  (49 shorter events, 4.6 us)
Async XLA Ops:
  6.5 227.0 %all-gather.4.cloned.1.call-start = ((), (), s32[]{:S(2)}) async-start(), calls=%async_computation.5 | async-start | bytes 28311552 | tf_op jit(solution)/shard_map/all_gather | solution.py:15
  7.3 1.1 copy-start
  7.3 452.1 %all-gather.6.cloned.1.call-start = ((), (), s32[]{:S(2)}) async-start(), calls=%async_computation.6 | async-start | bytes 28311552 | tf_op jit(solution)/shard_map/all_gather | solution.py:16
  8.0 17.3 %copy-start.1 = (f32[1,4,3,3072]{3,1,2,0:T(4,128)S(1)}, f32[1,4,3,3072]{3,1,2,0:T(4,128)}, u32[]{:S(2)}) copy-start(f32[1,4,3,3072]{3,1,2,0:T(4,128)} %param.11) | copy-start | bytes 442372
  8.0 492.1 %reduce-scatter.6.cloned.1.call-start = ((), (), s32[]{:S(2)}) async-start(), calls=%async_computation.7 | async-start | bytes 983040 | tf_op jit(solution)/shard_map/reduce_scatter | solution.py:47
  8.4 451.0 %copy-start.3 = (f32[1,3072]{1,0:T(1,128)S(1)}, f32[1,3072]{1,0:T(1,128)}, u32[]{:S(2)}) copy-start(f32[1,3072]{1,0:T(1,128)} %param.8) | copy-start | bytes 36868
  459.4 18.5 %copy-start.2 = (f32[1,768]{1,0:T(1,128)S(1)}, f32[1,768]{1,0:T(1,128)}, u32[]{:S(2)}) copy-start(f32[1,768]{1,0:T(1,128)} %param.10) | copy-start | bytes 9220
  477.8 86.0 %reduce-scatter.8.cloned.1.call-start = ((), (), s32[]{:S(2)}) async-start(), calls=%async_computation.8 | async-start | bytes 983040 | tf_op jit(solution)/shard_map/reduce_scatter | solution.py:47
  501.1 3.3 collective-permute-start
  540.4 87.3 %reduce-scatter.10.cloned.1.call-start = ((), (), s32[]{:S(2)}) async-start(), calls=%async_computation.9 | async-start | bytes 983040 | tf_op jit(solution)/shard_map/reduce_scatter | solution.py:47
  564.8 3.3 collective-permute-start.1
  604.2 87.3 %reduce-scatter.12.cloned.1.call-start = ((), (), s32[]{:S(2)}) async-start(), calls=%async_computation.10 | async-start | bytes 983040 | tf_op jit(solution)/shard_map/reduce_scatter | solution.py:47
  628.6 3.3 collective-permute-start.2
  668.0 87.3 %reduce-scatter.14.cloned.1.call-start = ((), (), s32[]{:S(2)}) async-start(), calls=%async_computation.11 | async-start | bytes 983040 | tf_op jit(solution)/shard_map/reduce_scatter | solution.py:47
  692.5 3.3 collective-permute-start.3
Sparse Core Ops, SparseCore 0:
  8.9 224.5 all-gather.3
  235.0 224.3 all-gather.5
  478.0 22.0 reduce-scatter.5
  540.5 23.2 reduce-scatter.7
  604.3 23.3 reduce-scatter.9
  668.1 23.2 reduce-scatter.11
  732.0 23.2 reduce-scatter.13
where the time goes:
time: 768 us; the launch traced here: 764 us
  waiting for transfers between devices  559 us (73%)
  matrix products  92.1 us (12%)
  blocking collectives  84.2 us (11%)
  between operations  13.6 us (2%)
  other arithmetic  8.14 us (1%)
    all_gather x1, waiting for transfers between devices, on_device(): lax.all_gather(w_out, 'col', axis=2, tiled=True)  226 us
    all_gather x1, waiting for transfers between devices, on_device(): lax.all_gather(w_in, 'col', axis=1, tiled=True)  208 us
    reduce_scatter x5, waiting for transfers between devices, on_device(): lax.psum_scatter(term.astype(jnp.bfloat16), 'row', scatter_dimension=1, t...  116 us
    dot_general x5, matrix products, on_device(): term = jnp.dot(hidden, w_second, preferred_element_type=jnp.float32)  92.1 us
    all_gather x5, blocking collectives, on_device(): whole = lax.all_gather(feed, 'row', axis=1, tiled=True).astype(jnp.float32)  84.2 us
  transfers between devices with their start and end apart: 11, of which 11 were waited for; matrix products, arithmetic and copies ran while one was open for 0% of the time, Pallas kernels for 0%

commit v1 on v0

--- a/solution.py
+++ b/solution.py
@@ -1,7 +1,17 @@
+import functools
+
 import jax
 import jax.numpy as jnp
 from jax import lax
+from jax.experimental import pallas as pl
+from jax.experimental.pallas import tpu as pltpu
 from jax.sharding import PartitionSpec as P
+
+MESH = pl.DeviceIdType.MESH
+ROWS = 4
+COLS = 2
+SEGS = 2
+BLOCK = 512
 
 
 def shifted(block, axis, distance):
@@ -10,7 +20,7 @@
     return lax.ppermute(block, axis, route)
 
 
-def on_device(latents, w_in, b_in, w_out, b_out, modulation):
+def general(latents, w_in, b_in, w_out, b_out, modulation):
     panels = (
         lax.all_gather(w_in, "col", axis=1, tiled=True),
         lax.all_gather(w_out, "col", axis=2, tiled=True),
@@ -54,7 +64,297 @@
     return chosen[None]
 
 
+def gelu(v):
+    return 0.5 * v * (1.0 + jnp.tanh(0.7978845608 * (v + 0.044715 * (v * v * v))))
+
+
+def kernel(
+    micros, blocks, own_ref, win_hbm, bin_ref, wout_hbm, bout_ref, shift_ref, scale_ref, gate_ref,
+    out_ref,
+    win, wout, feed, ready, pre, xsend, xrecv, total, psend, precv, ssend, srecv,
+    wsem, xs_sem, xr_sem, ss_sem, sr_sem, ps_sem, pr_sem, as_sem, ar_sem,
+):
+    row = lax.axis_index("row")
+    col = lax.axis_index("col")
+    seg = lax.axis_index("segment")
+    other_col = 1 - col
+    part = own_ref.shape[2]
+    half = part * ROWS
+
+    load_in = pltpu.make_async_copy(win_hbm, win, wsem.at[0])
+    load_out = pltpu.make_async_copy(wout_hbm, wout, wsem.at[1])
+    load_in.start()
+    load_out.start()
+
+    def row_at(k):
+        return lax.rem(row + k, ROWS)
+
+    barrier = pltpu.get_barrier_semaphore()
+    pl.semaphore_signal(barrier, inc=1, device_id={"col": other_col}, device_id_type=MESH)
+    for k in range(1, ROWS):
+        pl.semaphore_signal(barrier, inc=1, device_id={"row": row_at(k)}, device_id_type=MESH)
+    for k in range(ROWS):
+        pl.semaphore_signal(
+            barrier, inc=1, device_id={"row": row_at(k), "segment": 1 - seg}, device_id_type=MESH
+        )
+    pl.semaphore_wait(barrier, 2 * ROWS)
+
+    def exchange(m, j):
+        return pltpu.make_async_remote_copy(
+            src_ref=xsend.at[m, j], dst_ref=xrecv.at[m, j],
+            send_sem=xs_sem.at[m, j], recv_sem=xr_sem.at[m, j],
+            device_id={"col": other_col}, device_id_type=MESH,
+        )
+
+    def moments(m):
+        return pltpu.make_async_remote_copy(
+            src_ref=ssend.at[m], dst_ref=srecv.at[m],
+            send_sem=ss_sem.at[m], recv_sem=sr_sem.at[m],
+            device_id={"col": other_col}, device_id_type=MESH,
+        )
+
+    def partial(m, k):
+        return pltpu.make_async_remote_copy(
+            src_ref=psend.at[m, row_at(k)], dst_ref=precv.at[m, k],
+            send_sem=ps_sem.at[m, k], recv_sem=pr_sem.at[m, k],
+            device_id={"row": row_at(k)}, device_id_type=MESH,
+        )
+
+    def first_feed(m, k):
+        return pltpu.make_async_remote_copy(
+            src_ref=own_ref.at[m], dst_ref=feed.at[m, row],
+            send_sem=as_sem.at[m, k], recv_sem=ar_sem.at[m, k],
+            device_id={"row": row_at(k)}, device_id_type=MESH,
+        )
+
+    def next_feed(m, k):
+        return pltpu.make_async_remote_copy(
+            src_ref=out_ref.at[m], dst_ref=feed.at[m, row],
+            send_sem=as_sem.at[m, k], recv_sem=ar_sem.at[m, k],
+            device_id={"row": row_at(k), "segment": 1}, device_id_type=MESH,
+        )
+
+    def measure(m):
+        sums = jnp.zeros((feed.shape[2], 1), jnp.float32)
+        for q in range(ROWS):
+            sums += jnp.sum(feed[m, q].astype(jnp.float32), axis=-1, keepdims=True)
+        mean = sums / half
+        spread = jnp.zeros_like(sums)
+        for q in range(ROWS):
+            off = feed[m, q].astype(jnp.float32) - mean
+            spread += jnp.sum(off * off, axis=-1, keepdims=True)
+        lane = lax.broadcasted_iota(jnp.int32, ssend.shape[1:], 1)
+        ssend[m] = jnp.where(lane == 0, mean, spread)
+        moments(m).start()
+
+    def enter(m):
+        @pl.when(seg == 1)
+        def _():
+            for k in range(ROWS):
+                next_feed(m, k).wait_recv()
+            measure(m)
+
+        moments(m).wait_recv()
+        mine, theirs = ssend[m], srecv[m]
+        gap = mine[:, 0:1] - theirs[:, 0:1]
+        mean = 0.5 * (mine[:, 0:1] + theirs[:, 0:1])
+        var = (mine[:, 1:2] + theirs[:, 1:2] + (0.5 * half) * gap * gap) / (2 * half)
+        inverse = lax.rsqrt(var + 1e-06)
+        for q in range(ROWS):
+            at = pl.ds(q * part, part)
+            normed = (feed[m, q].astype(jnp.float32) - mean) * inverse
+            ready[:, at] = (
+                normed * (1.0 + scale_ref[m, :, at]) + shift_ref[m, :, at]
+            ).astype(jnp.bfloat16)
+
+        @pl.loop(0, blocks)
+        def _(j):
+            at = pl.ds(pl.multiple_of(j * BLOCK, BLOCK), BLOCK)
+            product = jnp.dot(ready[...], win[:, at], preferred_element_type=jnp.float32)
+            xsend[m, j] = product.astype(jnp.bfloat16)
+            exchange(m, j).start()
+            pre[lax.rem(m, 2), j] = product + bin_ref[:, at]
+
+    def middle(m):
+        total[...] = jnp.zeros_like(total)
+
+        @pl.loop(0, blocks)
+        def _(j):
+            exchange(m, j).wait_recv()
+            at = pl.ds(pl.multiple_of(j * BLOCK, BLOCK), BLOCK)
+            hidden = gelu(pre[lax.rem(m, 2), j] + xrecv[m, j].astype(jnp.float32))
+            total[...] += jnp.dot(
+                hidden.astype(jnp.bfloat16), wout[at, :], preferred_element_type=jnp.float32
+            )
+
+        for q in range(ROWS):
+            psend[m, q] = total[:, q * part:(q + 1) * part].astype(jnp.bfloat16)
+        for k in range(1, ROWS):
+            partial(m, k).start()
+
+    def leave(m):
+        branch = psend[m, row].astype(jnp.float32)
+        for k in range(1, ROWS):
+            partial(m, k).wait_recv()
+            branch += precv[m, k].astype(jnp.float32)
+        act = feed[m, row].astype(jnp.float32) + gate_ref[m] * (branch + bout_ref[...])
+        out_ref[m] = act.astype(jnp.bfloat16)
+
+        @pl.when(seg == 0)
+        def _():
+            for k in range(ROWS):
+                next_feed(m, k).start()
+
+    @pl.when(seg == 0)
+    def _():
+        @pl.loop(0, micros)
+        def _(m):
+            for k in range(1, ROWS):
+                first_feed(m, k).start()
+            feed[m, row] = own_ref[m]
+
+        @pl.loop(0, micros)
+        def _(m):
+            for k in range(1, ROWS):
+                first_feed(m, k).wait_recv()
+            measure(m)
+
+        @pl.loop(0, micros)
+        def _(m):
+            for k in range(1, ROWS):
+                first_feed(m, k).wait_send()
+
+    load_in.wait()
+    load_out.wait()
+
+    @pl.loop(0, micros + 2)
+    def _(i):
+        @pl.when(i >= 2)
+        def _():
+            leave(i - 2)
+
+        @pl.when(i < micros)
+        def _():
+            enter(i)
+
+        @pl.when((i >= 1) & (i <= micros))
+        def _():
+            middle(i - 1)
+
+    @pl.loop(0, micros)
+    def _(m):
+        moments(m).wait_send()
+        for k in range(1, ROWS):
+            partial(m, k).wait_send()
+
+        @pl.loop(0, blocks)
+        def _(j):
+            exchange(m, j).wait_send()
+
+        @pl.when(seg == 0)
+        def _():
+            for k in range(ROWS):
+                next_feed(m, k).wait_send()
+
+
+def layers(own, w_first, bias_first, w_second, bias_last, shift, scale, gate):
+    micros, tokens, part = own.shape
+    half, units = w_first.shape
+    blocks = units // BLOCK
+    vmem = pl.BlockSpec(memory_space=pltpu.VMEM)
+    hbm = pl.BlockSpec(memory_space=pl.ANY)
+    bf16, f32, dma = jnp.bfloat16, jnp.float32, pltpu.SemaphoreType.DMA
+    return pl.pallas_call(
+        functools.partial(kernel, micros, blocks),
+        out_shape=jax.ShapeDtypeStruct(own.shape, bf16),
+        in_specs=[vmem, hbm, vmem, hbm, vmem, vmem, vmem, vmem],
+        out_specs=vmem,
+        scratch_shapes=[
+            pltpu.VMEM((half, units), bf16),
+            pltpu.VMEM((units, half), bf16),
+            pltpu.VMEM((micros, ROWS, tokens, part), bf16),
+            pltpu.VMEM((tokens, half), bf16),
+            pltpu.VMEM((2, blocks, tokens, BLOCK), f32),
+            pltpu.VMEM((micros, blocks, tokens, BLOCK), bf16),
+            pltpu.VMEM((micros, blocks, tokens, BLOCK), bf16),
+            pltpu.VMEM((tokens, half), f32),
+            pltpu.VMEM((micros, ROWS, tokens, part), bf16),
+            pltpu.VMEM((micros, ROWS, tokens, part), bf16),
+            pltpu.VMEM((micros, tokens, 128), f32),
+            pltpu.VMEM((micros, tokens, 128), f32),
+            dma((2,)),
+            dma((micros, blocks)),
+            dma((micros, blocks)),
+            dma((micros,)),
+            dma((micros,)),
+            dma((micros, ROWS)),
+            dma((micros, ROWS)),
+            dma((micros, ROWS)),
+            dma((micros, ROWS)),
+        ],
+        compiler_params=pltpu.CompilerParams(
+            collective_id=0, has_side_effects=True, vmem_limit_bytes=62 * 1024 * 1024
+        ),
+        cost_estimate=pl.CostEstimate(
+            flops=4 * micros * tokens * half * units,
+            bytes_accessed=4 * half * units,
+            transcendentals=micros * tokens * units,
+        ),
+    )(own, w_first, bias_first, w_second, bias_last, shift, scale, gate)
+
+
+def stationary(latents, w_in, b_in, w_out, b_out, modulation):
+    row, col = lax.axis_index("row"), lax.axis_index("col")
+    width = latents.shape[2]
+    part = width // 2
+    here = latents.shape[1]
+    half = w_in.shape[1]
+
+    def place(r, c):
+        return r * COLS + c
+
+    def route(k):
+        return [
+            (place(r, c), place(2 * (r % 2) + (c + k) % 2, r // 2))
+            for r in range(ROWS) for c in range(COLS)
+        ]
+
+    parts = []
+    for k in range(2):
+        piece = lax.dynamic_slice_in_dim(latents, lax.rem(col + k, 2) * part, part, 2)
+        parts.append(lax.ppermute(piece, ("row", "col"), route(k)))
+    even = lax.rem(row, 2) == 0
+    own = jnp.concatenate(
+        [jnp.where(even, parts[0], parts[1]), jnp.where(even, parts[1], parts[0])], axis=1
+    )
+    bias_last = lax.ppermute(
+        lax.dynamic_slice_in_dim(b_out, col * part, part, 1), ("row", "col"), route(0)
+    )
+    mods = modulation[0]
+    shift = lax.dynamic_slice_in_dim(mods[:, 0:1], col * half, half, 2)
+    scale = lax.dynamic_slice_in_dim(mods[:, 1:2], col * half, half, 2)
+    gate = lax.dynamic_slice_in_dim(mods[:, 2:3], col * half + row * part, part, 2)
+    done = layers(own, w_in[0], b_in, w_out[0], bias_last, shift, scale, gate)
+    parts = []
+    for k in range(2):
+        piece = lax.dynamic_slice_in_dim(done, lax.rem(row + k, 2) * here, here, 1)
+        back = [(b, a) for a, b in route(k)]
+        parts.append(lax.ppermute(piece, ("row", "col"), back))
+    first = col == 0
+    return jnp.concatenate(
+        [jnp.where(first, parts[0], parts[1]), jnp.where(first, parts[1], parts[0])], axis=2
+    )[None]
+
+
 def solution(mesh):
+    sizes = dict(mesh.shape)
+    fits = (sizes["row"], sizes["col"], sizes["segment"]) == (ROWS, COLS, SEGS)
+
+    def on_device(latents, w_in, *rest):
+        aligned = latents.shape[2] % 256 == 0 and w_in.shape[2] % BLOCK == 0
+        chosen = stationary if fits and aligned else general
+        return chosen(latents, w_in, *rest)
+
     return jax.shard_map(
         on_device,
         mesh=mesh,

time: 768 us -> 272 us (0.35)
  waiting for transfers between devices: 559 us -> 30 us
  Pallas kernels: 0 us -> 225 us
  matrix products: 92.1 us -> 0 us
  blocking collectives: 84.2 us -> 0 us
  between operations: 13.6 us -> 0.14 us
    all_gather x2 -> x0, waiting for transfers between devices: 434 us -> none  [the longest x1 226 us: on_device(): lax.all_gather(w_out, 'col', axis=2, tiled=True)]
    pallas_call x0 -> x1, Pallas kernels: none -> 225 us  [layers(): pl.pallas_call(functools.partial(kernel, micros, blocks), out_shape=jax.S...]
    reduce_scatter x5 -> x0, waiting for transfers between devices: 116 us -> none  [on_device(): lax.psum_scatter(term.astype(jnp.bfloat16), 'row', scatter_dimension=1, t...]
    dot_general x5 -> x0, matrix products: 92.1 us -> none  [on_device(): term = jnp.dot(hidden, w_second, preferred_element_type=jnp.float32)]
    all_gather x5 -> x0, blocking collectives: 84.2 us -> none  [on_device(): whole = lax.all_gather(feed, 'row', axis=1, tiled=True).astype(jnp.float32)]
    ppermute x4 -> x5, waiting for transfers between devices: 8.14 us -> 30 us  [the longest x2 17.7 us: stationary(): parts.append(lax.ppermute(piece, ('row', 'col'), back))]
  transfers between devices with their start and end apart: 11 -> 5, of which waited for: 11 -> 4; matrix products, arithmetic and copies ran while one was open for 0% -> 1% of each run, Pallas kernels for 0% -> 0%
where the time goes in v1:
time: 272 us
  Pallas kernels  225 us (83%)
  waiting for transfers between devices  30 us (11%)
  starting transfers between devices  10.5 us (4%)
  local copies, waits for them, and re-layouts  4.47 us (2%)
    pallas_call x1, Pallas kernels, layers(): pl.pallas_call(functools.partial(kernel, micros, blocks), out_shape=jax.S...  225 us
    ppermute x2, waiting for transfers between devices, stationary(): parts.append(lax.ppermute(piece, ('row', 'col'), back))  17.7 us
    ppermute x2, waiting for transfers between devices, stationary(): parts.append(lax.ppermute(piece, ('row', 'col'), route(k)))  12.3 us
  transfers between devices with their start and end apart: 5, of which 4 were waited for; matrix products, arithmetic and copies ran while one was open for 1% of the time, Pallas kernels for 0%

profile of v1, /device:TPU:15, one launch (start us, length us, event | category | flops | bytes accessed | tf_op | source)
XLA Modules:
  0.0 272.1 jit_solution(7147182323122540336)
XLA Ops:
  0.0 0.0 copy-start
  0.0 0.0 copy-start.1
  0.0 1.2 constant_dynamic-slice_fusion.7
  1.3 4.2 %collective-permute-start = (bf16[4,128,384]{2,1,0:T(8,128)(2,1)S(1)}, bf16[4,128,384]{2,1,0:T(8,128)(2,1)S(1)}, u32[]{:S(2)}, u32[]{:S(2)}) collective-permute-start(bf16[4,128,384]{2,1,0:T(8,128)(2,1)S(1)} %get-tuple-element.11), channel_id=1, source_target_pairs={{0,0},{2,4},{4,8},{6,12},{8,2},{10,6},{12,10},{14,14},{1,1},{3,5},... | collective-permute-start | bytes 1179656 | tf_op jit(solution)/shard_map/ppermute | solution.py:325
  5.4 0.1 collective-permute-start.1
  5.5 0.0 copy-done
  5.5 3.0 %collective-permute-start.2 = (f32[1,384]{1,0:T(1,128)S(1)}, f32[1,384]{1,0:T(1,128)S(1)}, u32[]{:S(2)}, u32[]{:S(2)}) collective-permute-start(f32[1,384]{1,0:T(1,128)S(1)} %constant_dynamic-slice_fusion.5), channel_id=1, source_target_pairs={{0,0},{2,4},{4,8},{6,12},{8,2},{10,6},{12,10},{14,14},{1,1},{3,5},... | collective-permute-start | bytes 4616 | tf_op jit(solution)/shard_map/ppermute | solution.py:330
  8.6 0.0 copy-done.1
  8.6 0.1 copy.9
  8.7 0.1 fusion
  8.8 0.6 constant_dynamic-slice_fusion.2.gate_ref
  9.4 0.6 constant_dynamic-slice_fusion.3
  10.0 3.2 %collective-permute-done = bf16[4,128,384]{2,1,0:T(8,128)(2,1)S(1)} collective-permute-done((bf16[4,128,384]{2,1,0:T(8,128)(2,1)S(1)}, bf16[4,128,384]{2,1,0:T(8,128)(2,1)S(1)}, u32[]{:S(2)}, u32[]{:S(2)}) %collective-permute-start) | collective-permute-done | bytes 393248 | tf_op jit(solution)/shard_map/ppermute | solution.py:325
  13.2 9.1 %collective-permute-done.1 = bf16[4,128,384]{2,1,0:T(8,128)(2,1)S(1)} collective-permute-done((bf16[4,128,384]{2,1,0:T(8,128)(2,1)S(1)}, bf16[4,128,384]{2,1,0:T(8,128)(2,1)S(1)}, u32[]{:S(2)}, u32[]{:S(2)}) %collective-permute-start.1) | collective-permute-done | bytes 393248 | tf_op jit(solution)/shard_map/ppermute | solution.py:325
  22.3 0.1 broadcast_select_fusion.1
  22.4 1.0 pad_maximum_fusion.own_ref
  23.4 0.0 collective-permute-done.2.bout_ref
  23.4 0.0 copy-start.2
  23.4 0.6 copy-done.2
  24.0 224.9 %shard_map.64 = bf16[4,256,384]{2,1,0:T(8,128)(2,1)} custom-call(bf16[4,256,384]{2,1,0:T(8,128)(2,1)} %pad_maximum_fusion.own_ref, bf16[1536,3072]{1,0:T(8,128)(2,1)} %bitcast.8, f32[1,3072]{1,0:T(1,128)} %bin_ref.1, bf16[3072,1536]{1,0:T(8,128)(2,1)} %bitcast.9, f32[1,384]{1,0:T(1,128)} %copy-done.2, f32[4,1,1536]{2,1,0:T(1,128)} %get-tuple-element.17.shift_ref, ...), custom_call_target="tpu_custom_call" | custom-call | flops 19327352832 | bytes 18874368 | tf_op jit(solution)/shard_map/pallas_call | solution.py:267
  248.8 1.2 constant_dynamic-slice_fusion.1
  250.1 3.1 %collective-permute-start.3 = (bf16[4,128,384]{2,1,0:T(8,128)(2,1)S(1)}, bf16[4,128,384]{2,1,0:T(8,128)(2,1)S(1)}, u32[]{:S(2)}, u32[]{:S(2)}) collective-permute-start(bf16[4,128,384]{2,1,0:T(8,128)(2,1)S(1)} %get-tuple-element.7), channel_id=1, source_target_pairs={{0,0},{4,2},{8,4},{12,6},{2,8},{6,10},{10,12},{14,14},{1,1},{5,3},... | collective-permute-start | bytes 1179656 | tf_op jit(solution)/shard_map/ppermute | solution.py:342
  253.2 0.2 collective-permute-start.4
  253.4 11.8 %collective-permute-done.3 = bf16[4,128,384]{2,1,0:T(8,128)(2,1)S(1)} collective-permute-done((bf16[4,128,384]{2,1,0:T(8,128)(2,1)S(1)}, bf16[4,128,384]{2,1,0:T(8,128)(2,1)S(1)}, u32[]{:S(2)}, u32[]{:S(2)}) %collective-permute-start.3) | collective-permute-done | bytes 393248 | tf_op jit(solution)/shard_map/ppermute | solution.py:342
  265.2 5.9 %collective-permute-done.4 = bf16[4,128,384]{2,1,0:T(8,128)(2,1)S(1)} collective-permute-done((bf16[4,128,384]{2,1,0:T(8,128)(2,1)S(1)}, bf16[4,128,384]{2,1,0:T(8,128)(2,1)S(1)}, u32[]{:S(2)}, u32[]{:S(2)}) %collective-permute-start.4) | collective-permute-done | bytes 393248 | tf_op jit(solution)/shard_map/ppermute | solution.py:342
  271.1 0.1 broadcast_select_fusion.3
  271.2 0.9 maximum_bitcast_fusion
  (1 shorter events, 0.0 us)
Async XLA Ops:
  0.0 5.5 %copy-start = (f32[1,768]{1,0:T(1,128)S(1)}, f32[1,768]{1,0:T(1,128)}, u32[]{:S(2)}) copy-start(f32[1,768]{1,0:T(1,128)} %param.10) | copy-start | bytes 9220
  0.0 8.6 %copy-start.1 = (f32[1,4,3,3072]{3,1,2,0:T(4,128)S(1)}, f32[1,4,3,3072]{3,1,2,0:T(4,128)}, u32[]{:S(2)}) copy-start(f32[1,4,3,3072]{3,1,2,0:T(4,128)} %param.11) | copy-start | bytes 442372
  1.3 12.0 %collective-permute-start = (bf16[4,128,384]{2,1,0:T(8,128)(2,1)S(1)}, bf16[4,128,384]{2,1,0:T(8,128)(2,1)S(1)}, u32[]{:S(2)}, u32[]{:S(2)}) collective-permute-start(bf16[4,128,384]{2,1,0:T(8,128)(2,1)S(1)} %get-tuple-element.11), channel_id=1, source_target_pairs={{0,0},{2,4},{4,8},{6,12},{8,2},{10,6},{12,10},{14,14},{1,1},{3,5},... | collective-permute-start | bytes 1179656 | tf_op jit(solution)/shard_map/ppermute | solution.py:325
  5.4 16.9 %collective-permute-start.1 = (bf16[4,128,384]{2,1,0:T(8,128)(2,1)S(1)}, bf16[4,128,384]{2,1,0:T(8,128)(2,1)S(1)}, u32[]{:S(2)}, u32[]{:S(2)}) collective-permute-start(bf16[4,128,384]{2,1,0:T(8,128)(2,1)S(1)} %get-tuple-element.12), channel_id=1, source_target_pairs={{0,4},{2,0},{4,12},{6,8},{8,6},{10,2},{12,14},{14,10},{1,5},{3,1},... | collective-permute-start | bytes 1179656 | tf_op jit(solution)/shard_map/ppermute | solution.py:325
  5.5 17.8 %collective-permute-start.2 = (f32[1,384]{1,0:T(1,128)S(1)}, f32[1,384]{1,0:T(1,128)S(1)}, u32[]{:S(2)}, u32[]{:S(2)}) collective-permute-start(f32[1,384]{1,0:T(1,128)S(1)} %constant_dynamic-slice_fusion.5), channel_id=1, source_target_pairs={{0,0},{2,4},{4,8},{6,12},{8,2},{10,6},{12,10},{14,14},{1,1},{3,5},... | collective-permute-start | bytes 4616 | tf_op jit(solution)/shard_map/ppermute | solution.py:330
  23.4 0.6 copy-start.2
  250.1 15.1 %collective-permute-start.3 = (bf16[4,128,384]{2,1,0:T(8,128)(2,1)S(1)}, bf16[4,128,384]{2,1,0:T(8,128)(2,1)S(1)}, u32[]{:S(2)}, u32[]{:S(2)}) collective-permute-start(bf16[4,128,384]{2,1,0:T(8,128)(2,1)S(1)} %get-tuple-element.7), channel_id=1, source_target_pairs={{0,0},{4,2},{8,4},{12,6},{2,8},{6,10},{10,12},{14,14},{1,1},{5,3},... | collective-permute-start | bytes 1179656 | tf_op jit(solution)/shard_map/ppermute | solution.py:342
  253.2 17.9 %collective-permute-start.4 = (bf16[4,128,384]{2,1,0:T(8,128)(2,1)S(1)}, bf16[4,128,384]{2,1,0:T(8,128)(2,1)S(1)}, u32[]{:S(2)}, u32[]{:S(2)}) collective-permute-start(bf16[4,128,384]{2,1,0:T(8,128)(2,1)S(1)} %get-tuple-element.8), channel_id=1, source_target_pairs={{4,0},{0,2},{12,4},{8,6},{6,8},{2,10},{14,12},{10,14},{5,1},{1,3},... | collective-permute-start | bytes 1179656 | tf_op jit(solution)/shard_map/ppermute | solution.py:342

commit v2 on v1

--- a/solution.py
+++ b/solution.py
@@ -69,16 +69,17 @@
 
 
 def kernel(
-    micros, blocks, own_ref, win_hbm, bin_ref, wout_hbm, bout_ref, shift_ref, scale_ref, gate_ref,
+    micros, blocks, lat_ref, win_hbm, bin_ref, wout_hbm, bout_ref, mods_ref,
     out_ref,
-    win, wout, feed, ready, pre, xsend, xrecv, total, psend, precv, ssend, srecv,
+    win, wout, feed, ready, pre, xsend, xrecv, total, psend, precv, ssend, srecv, result, landed, bout,
     wsem, xs_sem, xr_sem, ss_sem, sr_sem, ps_sem, pr_sem, as_sem, ar_sem,
+    is_sem, ir_sem, os_sem, or_sem, bs_sem, br_sem,
 ):
     row = lax.axis_index("row")
     col = lax.axis_index("col")
     seg = lax.axis_index("segment")
-    other_col = 1 - col
-    part = own_ref.shape[2]
+    here, width = lat_ref.shape[1:]
+    part = width // 2
     half = part * ROWS
 
     load_in = pltpu.make_async_copy(win_hbm, win, wsem.at[0])
@@ -89,28 +90,40 @@
     def row_at(k):
         return lax.rem(row + k, ROWS)
 
+    placed_row = 2 * col + row // 2
+    work_col = row // 2
+
+    def work_row(h):
+        return 2 * lax.rem(row, 2) + h
+
+    def works_own(h):
+        return (work_row(h) == row) & (work_col == col)
+
     barrier = pltpu.get_barrier_semaphore()
-    pl.semaphore_signal(barrier, inc=1, device_id={"col": other_col}, device_id_type=MESH)
-    for k in range(1, ROWS):
-        pl.semaphore_signal(barrier, inc=1, device_id={"row": row_at(k)}, device_id_type=MESH)
     for k in range(ROWS):
-        pl.semaphore_signal(
-            barrier, inc=1, device_id={"row": row_at(k), "segment": 1 - seg}, device_id_type=MESH
-        )
-    pl.semaphore_wait(barrier, 2 * ROWS)
+        for c in range(COLS):
+            for g in range(SEGS):
+                if k or c or g:
+                    pl.semaphore_signal(
+                        barrier, inc=1, device_id_type=MESH,
+                        device_id={
+                            "row": row_at(k), "col": lax.rem(col + c, COLS), "segment": lax.rem(seg + g, SEGS)
+                        },
+                    )
+    pl.semaphore_wait(barrier, ROWS * COLS * SEGS - 1)
 
     def exchange(m, j):
         return pltpu.make_async_remote_copy(
             src_ref=xsend.at[m, j], dst_ref=xrecv.at[m, j],
             send_sem=xs_sem.at[m, j], recv_sem=xr_sem.at[m, j],
-            device_id={"col": other_col}, device_id_type=MESH,
+            device_id={"col": 1 - col}, device_id_type=MESH,
         )
 
     def moments(m):
         return pltpu.make_async_remote_copy(
             src_ref=ssend.at[m], dst_ref=srecv.at[m],
             send_sem=ss_sem.at[m], recv_sem=sr_sem.at[m],
-            device_id={"col": other_col}, device_id_type=MESH,
+            device_id={"col": 1 - col}, device_id_type=MESH,
         )
 
     def partial(m, k):
@@ -122,19 +135,76 @@
 
     def first_feed(m, k):
         return pltpu.make_async_remote_copy(
-            src_ref=own_ref.at[m], dst_ref=feed.at[m, row],
+            src_ref=feed.at[m, row], dst_ref=feed.at[m, row],
             send_sem=as_sem.at[m, k], recv_sem=ar_sem.at[m, k],
             device_id={"row": row_at(k)}, device_id_type=MESH,
         )
 
     def next_feed(m, k):
         return pltpu.make_async_remote_copy(
-            src_ref=out_ref.at[m], dst_ref=feed.at[m, row],
+            src_ref=result.at[m], dst_ref=feed.at[m, row],
             send_sem=as_sem.at[m, k], recv_sem=ar_sem.at[m, k],
             device_id={"row": row_at(k), "segment": 1}, device_id_type=MESH,
         )
 
+    def mine_at(c):
+        return pl.ds(pl.multiple_of(c * here, here), here)
+
+    def latent(m, h, c):
+        return pltpu.make_async_remote_copy(
+            src_ref=lat_ref.at[m, :, pl.ds(h * part, part)],
+            dst_ref=feed.at[m, work_row(h), mine_at(col)],
+            send_sem=is_sem.at[m, h], recv_sem=ir_sem.at[m, c],
+            device_id={"row": work_row(h), "col": work_col}, device_id_type=MESH,
+        )
+
+    def finished(m, c, h):
+        at = pl.ds(pl.multiple_of(lax.rem(row, 2) * part, 128), part)
+        return pltpu.make_async_remote_copy(
+            src_ref=result.at[m, pl.ds(c * here, here)],
+            dst_ref=landed.at[m, :, at],
+            send_sem=os_sem.at[m, c], recv_sem=or_sem.at[m, h],
+            device_id={"row": placed_row, "col": c}, device_id_type=MESH,
+        )
+
+    def last_bias():
+        return pltpu.make_async_remote_copy(
+            src_ref=bout_ref.at[:, pl.ds(pl.multiple_of(col * part, 128), part)], dst_ref=bout,
+            send_sem=bs_sem.at[0], recv_sem=br_sem.at[0],
+            device_id={"row": work_row(col), "col": work_col}, device_id_type=MESH,
+        )
+
+    def send_latents(m):
+        for h in range(2):
+            own = works_own(h)
+
+            @pl.when(own)
+            def _():
+                feed[m, row, mine_at(col)] = lat_ref[m, :, h * part:(h + 1) * part]
+
+            @pl.when(jnp.logical_not(own))
+            def _():
+                latent(m, h, col).start()
+
+    def spread_latents(m):
+        for c in range(COLS):
+            @pl.when(jnp.logical_not((placed_row == row) & (col == c)))
+            def _():
+                latent(m, 0, c).wait_recv()
+        for k in range(1, ROWS):
+            first_feed(m, k).start()
+
     def measure(m):
+        @pl.when(seg == 0)
+        def _():
+            for k in range(1, ROWS):
+                first_feed(m, k).wait_recv()
+
+        @pl.when(seg == 1)
+        def _():
+            for k in range(ROWS):
+                next_feed(m, k).wait_recv()
+
         sums = jnp.zeros((feed.shape[2], 1), jnp.float32)
         for q in range(ROWS):
             sums += jnp.sum(feed[m, q].astype(jnp.float32), axis=-1, keepdims=True)
@@ -148,12 +218,6 @@
         moments(m).start()
 
     def enter(m):
-        @pl.when(seg == 1)
-        def _():
-            for k in range(ROWS):
-                next_feed(m, k).wait_recv()
-            measure(m)
-
         moments(m).wait_recv()
         mine, theirs = ssend[m], srecv[m]
         gap = mine[:, 0:1] - theirs[:, 0:1]
@@ -161,11 +225,15 @@
         var = (mine[:, 1:2] + theirs[:, 1:2] + (0.5 * half) * gap * gap) / (2 * half)
         inverse = lax.rsqrt(var + 1e-06)
         for q in range(ROWS):
-            at = pl.ds(q * part, part)
+            at = pl.ds(pl.multiple_of(col * half + q * part, 128), part)
             normed = (feed[m, q].astype(jnp.float32) - mean) * inverse
-            ready[:, at] = (
-                normed * (1.0 + scale_ref[m, :, at]) + shift_ref[m, :, at]
+            ready[:, q * part:(q + 1) * part] = (
+                normed * (1.0 + mods_ref[m, 1:2, at]) + mods_ref[m, 0:1, at]
             ).astype(jnp.bfloat16)
+
+        @pl.when((m + 1 < micros) & ((seg == 1) | (m >= 1)))
+        def _():
+            measure(m + 1)
 
         @pl.loop(0, blocks)
         def _(j):
@@ -174,6 +242,16 @@
             xsend[m, j] = product.astype(jnp.bfloat16)
             exchange(m, j).start()
             pre[lax.rem(m, 2), j] = product + bin_ref[:, at]
+
+        @pl.when(seg == 0)
+        def _():
+            @pl.when((m == 0) & (micros > 1))
+            def _():
+                measure(m + 1)
+
+            @pl.when(m + 2 < micros)
+            def _():
+                spread_latents(m + 2)
 
     def middle(m):
         total[...] = jnp.zeros_like(total)
@@ -197,52 +275,89 @@
         for k in range(1, ROWS):
             partial(m, k).wait_recv()
             branch += precv[m, k].astype(jnp.float32)
-        act = feed[m, row].astype(jnp.float32) + gate_ref[m] * (branch + bout_ref[...])
-        out_ref[m] = act.astype(jnp.bfloat16)
+        at = pl.ds(pl.multiple_of(col * half + row * part, 128), part)
+        act = feed[m, row].astype(jnp.float32) + mods_ref[m, 2:3, at] * (branch + bout[0:1, :])
+        result[m] = act.astype(jnp.bfloat16)
 
         @pl.when(seg == 0)
         def _():
             for k in range(ROWS):
                 next_feed(m, k).start()
+
+        for c in range(COLS):
+            own = (placed_row == row) & (col == c)
+
+            @pl.when(jnp.logical_not(own))
+            def _():
+                finished(m, c, lax.rem(row, 2)).start()
+
+            for h in range(2):
+                @pl.when(own & (lax.rem(row, 2) == h))
+                def _():
+                    landed[m, :, h * part:(h + 1) * part] = result[m, c * here:(c + 1) * here]
 
     @pl.when(seg == 0)
     def _():
         @pl.loop(0, micros)
         def _(m):
-            for k in range(1, ROWS):
-                first_feed(m, k).start()
-            feed[m, row] = own_ref[m]
-
-        @pl.loop(0, micros)
-        def _(m):
-            for k in range(1, ROWS):
-                first_feed(m, k).wait_recv()
-            measure(m)
-
-        @pl.loop(0, micros)
-        def _(m):
-            for k in range(1, ROWS):
-                first_feed(m, k).wait_send()
-
+            send_latents(m)
+
+    own_bias = works_own(col)
+
+    @pl.when(own_bias)
+    def _():
+        for h in range(2):
+            @pl.when(col == h)
+            def _():
+                bout[...] = bout_ref[:, h * part:(h + 1) * part]
+
+    @pl.when(jnp.logical_not(own_bias))
+    def _():
+        last_bias().start()
+
+    @pl.when(seg == 0)
+    def _():
+        spread_latents(0)
+        if micros > 1:
+            spread_latents(1)
+
+    measure(0)
     load_in.wait()
-    load_out.wait()
 
     @pl.loop(0, micros + 2)
     def _(i):
+        @pl.when(i < micros)
+        def _():
+            enter(i)
+
+        @pl.when(i == 1)
+        def _():
+            load_out.wait()
+
+            @pl.when(jnp.logical_not((placed_row == row) & (lax.rem(row, 2) == col)))
+            def _():
+                last_bias().wait_recv()
+
         @pl.when(i >= 2)
         def _():
             leave(i - 2)
 
-        @pl.when(i < micros)
-        def _():
-            enter(i)
-
         @pl.when((i >= 1) & (i <= micros))
         def _():
             middle(i - 1)
+
+    @pl.when(jnp.logical_not(own_bias))
+    def _():
+        last_bias().wait_send()
 
     @pl.loop(0, micros)
     def _(m):
+        for h in range(2):
+            @pl.when(jnp.logical_not(works_own(h)))
+            def _():
+                finished(m, 0, h).wait_recv()
+
+        out_ref[m] = landed[m]
         moments(m).wait_send()
         for k in range(1, ROWS):
             partial(m, k).wait_send()
@@ -251,23 +366,35 @@
         def _(j):
             exchange(m, j).wait_send()
 
+        for c in range(COLS):
+            @pl.when(jnp.logical_not((placed_row == row) & (col == c)))
+            def _():
+                finished(m, c, 0).wait_send()
+
         @pl.when(seg == 0)
         def _():
             for k in range(ROWS):
                 next_feed(m, k).wait_send()
-
-
-def layers(own, w_first, bias_first, w_second, bias_last, shift, scale, gate):
-    micros, tokens, part = own.shape
-    half, units = w_first.shape
+            for k in range(1, ROWS):
+                first_feed(m, k).wait_send()
+            for h in range(2):
+                @pl.when(jnp.logical_not(works_own(h)))
+                def _():
+                    latent(m, h, 0).wait_send()
+
+
+def stationary(latents, w_in, b_in, w_out, b_out, modulation):
+    micros, here, width = latents.shape
+    tokens, part = COLS * here, width // 2
+    half, units = w_in.shape[1:]
     blocks = units // BLOCK
     vmem = pl.BlockSpec(memory_space=pltpu.VMEM)
     hbm = pl.BlockSpec(memory_space=pl.ANY)
     bf16, f32, dma = jnp.bfloat16, jnp.float32, pltpu.SemaphoreType.DMA
-    return pl.pallas_call(
+    done = pl.pallas_call(
         functools.partial(kernel, micros, blocks),
-        out_shape=jax.ShapeDtypeStruct(own.shape, bf16),
-        in_specs=[vmem, hbm, vmem, hbm, vmem, vmem, vmem, vmem],
+        out_shape=jax.ShapeDtypeStruct(latents.shape, bf16),
+        in_specs=[vmem, hbm, vmem, hbm, vmem, vmem],
         out_specs=vmem,
         scratch_shapes=[
             pltpu.VMEM((half, units), bf16),
@@ -282,6 +409,9 @@
             pltpu.VMEM((micros, ROWS, tokens, part), bf16),
             pltpu.VMEM((micros, tokens, 128), f32),
             pltpu.VMEM((micros, tokens, 128), f32),
+            pltpu.VMEM((micros, tokens, part), bf16),
+            pltpu.VMEM((micros, here, width), bf16),
+            pltpu.VMEM((8, part), f32),
             dma((2,)),
             dma((micros, blocks)),
             dma((micros, blocks)),
@@ -291,6 +421,12 @@
             dma((micros, ROWS)),
             dma((micros, ROWS)),
             dma((micros, ROWS)),
+            dma((micros, 2)),
+            dma((micros, COLS)),
+            dma((micros, COLS)),
+            dma((micros, 2)),
+            dma((1,)),
+            dma((1,)),
         ],
         compiler_params=pltpu.CompilerParams(
             collective_id=0, has_side_effects=True, vmem_limit_bytes=62 * 1024 * 1024
@@ -300,50 +436,8 @@
             bytes_accessed=4 * half * units,
             transcendentals=micros * tokens * units,
         ),
-    )(own, w_first, bias_first, w_second, bias_last, shift, scale, gate)
-
-
-def stationary(latents, w_in, b_in, w_out, b_out, modulation):
-    row, col = lax.axis_index("row"), lax.axis_index("col")
-    width = latents.shape[2]
-    part = width // 2
-    here = latents.shape[1]
-    half = w_in.shape[1]
-
-    def place(r, c):
-        return r * COLS + c
-
-    def route(k):
-        return [
-            (place(r, c), place(2 * (r % 2) + (c + k) % 2, r // 2))
-            for r in range(ROWS) for c in range(COLS)
-        ]
-
-    parts = []
-    for k in range(2):
-        piece = lax.dynamic_slice_in_dim(latents, lax.rem(col + k, 2) * part, part, 2)
-        parts.append(lax.ppermute(piece, ("row", "col"), route(k)))
-    even = lax.rem(row, 2) == 0
-    own = jnp.concatenate(
-        [jnp.where(even, parts[0], parts[1]), jnp.where(even, parts[1], parts[0])], axis=1
-    )
-    bias_last = lax.ppermute(
-        lax.dynamic_slice_in_dim(b_out, col * part, part, 1), ("row", "col"), route(0)
-    )
-    mods = modulation[0]
-    shift = lax.dynamic_slice_in_dim(mods[:, 0:1], col * half, half, 2)
-    scale = lax.dynamic_slice_in_dim(mods[:, 1:2], col * half, half, 2)
-    gate = lax.dynamic_slice_in_dim(mods[:, 2:3], col * half + row * part, part, 2)
-    done = layers(own, w_in[0], b_in, w_out[0], bias_last, shift, scale, gate)
-    parts = []
-    for k in range(2):
-        piece = lax.dynamic_slice_in_dim(done, lax.rem(row + k, 2) * here, here, 1)
-        back = [(b, a) for a, b in route(k)]
-        parts.append(lax.ppermute(piece, ("row", "col"), back))
-    first = col == 0
-    return jnp.concatenate(
-        [jnp.where(first, parts[0], parts[1]), jnp.where(first, parts[1], parts[0])], axis=2
-    )[None]
+    )(latents, w_in[0], b_in, w_out[0], jnp.broadcast_to(b_out, (8, width)), modulation[0])
+    return done[None]
 
 
 def solution(mesh):

time: 272 us -> 227 us (0.83)
  waiting for transfers between devices: 30 us -> 0 us
  starting transfers between devices: 10.5 us -> 0 us
  Pallas kernels: 225 us -> 221 us
    ppermute x5 -> x0, waiting for transfers between devices: 30 us -> none  [the longest x2 17.7 us: stationary(): parts.append(lax.ppermute(piece, ('row', 'col'), back))]
    ppermute x5 -> x0, starting transfers between devices: 10.5 us -> none  [the longest x2 4.25 us: stationary(): parts.append(lax.ppermute(piece, ('row', 'col'), route(k)))]
    dynamic_slice x5 -> x0, local copies, waits for them, and re-layouts: 3.68 us -> none  [the longest x1 1.24 us: stationary(): lax.dynamic_slice_in_dim(latents, lax.rem(col + k, 2) * part, part, 2)]
    pallas_call x1, Pallas kernels: 225 us -> 221 us  [stationary(): pl.pallas_call(functools.partial(kernel, micros, blocks), out_shape=jax.S...]
    unnamed x7 -> x2, local copies, waits for them, and re-layouts: 0.69 us -> 3.75 us
  transfers between devices with their start and end apart: 5 -> 0, of which waited for: 4 -> 0; matrix products, arithmetic and copies ran while one was open for 1% -> 0% of each run, Pallas kernels for 0% -> 0%
where the time goes in v2:
time: 227 us; the launch traced here: 226 us
  Pallas kernels  221 us (97%)
  local copies, waits for them, and re-layouts  4.35 us (2%)
    pallas_call x1, Pallas kernels, stationary(): pl.pallas_call(functools.partial(kernel, micros, blocks), out_shape=jax.S...  221 us

profile of v2, /device:TPU:15, one launch (start us, length us, event | category | flops | bytes accessed | tf_op | source)
XLA Modules:
  0.0 226.3 jit_solution(3993915750721946228)
XLA Ops:
  0.0 0.7 reduce
  0.7 0.6 broadcast_in_dim.11.bout_ref
  1.3 1.7 copy.9
  3.0 221.3 %shard_map.64 = bf16[4,128,768]{2,1,0:T(8,128)(2,1)} custom-call(bf16[4,128,768]{2,1,0:T(8,128)(2,1)} %lat_ref.1, bf16[1536,3072]{1,0:T(8,128)(2,1)} %bitcast.8, f32[1,3072]{1,0:T(1,128)} %bin_ref.1, bf16[3072,1536]{1,0:T(8,128)(2,1)} %bitcast.9, f32[8,768]{1,0:T(8,128)} %broadcast_in_dim.11.bout_ref, f32[4,3,3072]{2,1,0:T(4,128)} %bitcast.7), custom_call_target="tpu_custom_call" | custom-call | flops 19327352832 | bytes 18874368 | tf_op jit(solution)/shard_map/pallas_call | solution.py:394
  224.3 2.1 copy.11

commit v3 on v2

--- a/solution.py
+++ b/solution.py
@@ -73,7 +73,7 @@
     out_ref,
     win, wout, feed, ready, pre, xsend, xrecv, total, psend, precv, ssend, srecv, result, landed, bout,
     wsem, xs_sem, xr_sem, ss_sem, sr_sem, ps_sem, pr_sem, as_sem, ar_sem,
-    is_sem, ir_sem, os_sem, or_sem, bs_sem, br_sem,
+    is_sem, ir_sem, os_sem, or_sem, bs_sem, br_sem, fs_sem, ns_sem,
 ):
     row = lax.axis_index("row")
     col = lax.axis_index("col")
@@ -133,18 +133,31 @@
             device_id={"row": row_at(k)}, device_id_type=MESH,
         )
 
-    def first_feed(m, k):
+    partner = row + 1 - 2 * lax.rem(row, 2)
+    across = 2 - row // 2
+    beyond = 2 - 2 * (row // 2)
+    hands_on = (row == 1) | (row == 2)
+    targets = (row, partner, across)
+
+    def first_feed(m, i):
         return pltpu.make_async_remote_copy(
             src_ref=feed.at[m, row], dst_ref=feed.at[m, row],
-            send_sem=as_sem.at[m, k], recv_sem=ar_sem.at[m, k],
-            device_id={"row": row_at(k)}, device_id_type=MESH,
-        )
-
-    def next_feed(m, k):
+            send_sem=ns_sem.at[m, i], recv_sem=ar_sem.at[m, row],
+            device_id={"row": targets[i]}, device_id_type=MESH,
+        )
+
+    def next_feed(m, i):
         return pltpu.make_async_remote_copy(
             src_ref=result.at[m], dst_ref=feed.at[m, row],
-            send_sem=as_sem.at[m, k], recv_sem=ar_sem.at[m, k],
-            device_id={"row": row_at(k), "segment": 1}, device_id_type=MESH,
+            send_sem=as_sem.at[m, i], recv_sem=ar_sem.at[m, row],
+            device_id={"row": targets[i], "segment": 1}, device_id_type=MESH,
+        )
+
+    def passed(m, q, i):
+        return pltpu.make_async_remote_copy(
+            src_ref=feed.at[m, q], dst_ref=feed.at[m, q],
+            send_sem=fs_sem.at[m, i], recv_sem=ar_sem.at[m, q],
+            device_id={"row": partner}, device_id_type=MESH,
         )
 
     def mine_at(c):
@@ -191,19 +204,22 @@
             @pl.when(jnp.logical_not((placed_row == row) & (col == c)))
             def _():
                 latent(m, 0, c).wait_recv()
-        for k in range(1, ROWS):
-            first_feed(m, k).start()
+        for i in (2, 1):
+            first_feed(m, i).start()
 
     def measure(m):
-        @pl.when(seg == 0)
-        def _():
-            for k in range(1, ROWS):
-                first_feed(m, k).wait_recv()
+        for i in range(2):
+            passed(m, beyond + i, i).wait_recv()
+
+            @pl.when(hands_on)
+            def _():
+                passed(m, beyond + i, i).start()
+
+        passed(m, partner, 0).wait_recv()
 
         @pl.when(seg == 1)
         def _():
-            for k in range(ROWS):
-                next_feed(m, k).wait_recv()
+            passed(m, row, 0).wait_recv()
 
         sums = jnp.zeros((feed.shape[2], 1), jnp.float32)
         for q in range(ROWS):
@@ -281,8 +297,8 @@
 
         @pl.when(seg == 0)
         def _():
-            for k in range(ROWS):
-                next_feed(m, k).start()
+            for i in (2, 1, 0):
+                next_feed(m, i).start()
 
         for c in range(COLS):
             own = (placed_row == row) & (col == c)
@@ -371,12 +387,17 @@
             def _():
                 finished(m, c, 0).wait_send()
 
+        @pl.when(hands_on)
+        def _():
+            for i in range(2):
+                passed(m, beyond + i, i).wait_send()
+
         @pl.when(seg == 0)
         def _():
-            for k in range(ROWS):
-                next_feed(m, k).wait_send()
-            for k in range(1, ROWS):
-                first_feed(m, k).wait_send()
+            for i in range(3):
+                next_feed(m, i).wait_send()
+            for i in (1, 2):
+                first_feed(m, i).wait_send()
             for h in range(2):
                 @pl.when(jnp.logical_not(works_own(h)))
                 def _():
@@ -427,6 +448,8 @@
             dma((micros, 2)),
             dma((1,)),
             dma((1,)),
+            dma((micros, 2)),
+            dma((micros, ROWS)),
         ],
         compiler_params=pltpu.CompilerParams(
             collective_id=0, has_side_effects=True, vmem_limit_bytes=62 * 1024 * 1024

time: 227 us -> 218 us (0.960)
  Pallas kernels: 221 us -> 213 us
    pallas_call x1, Pallas kernels: 221 us -> 213 us  [stationary(): pl.pallas_call(functools.partial(kernel, micros, blocks), out_shape=jax.S...]
where the time goes in v3:
time: 218 us
  Pallas kernels  213 us (98%)
  local copies, waits for them, and re-layouts  4.35 us (2%)
    pallas_call x1, Pallas kernels, stationary(): pl.pallas_call(functools.partial(kernel, micros, blocks), out_shape=jax.S...  213 us

profile of v3, /device:TPU:15, one launch (start us, length us, event | category | flops | bytes accessed | tf_op | source)
XLA Modules:
  0.0 218.2 jit_solution(7196327534424654591)
XLA Ops:
  0.0 0.7 reduce
  0.7 0.6 broadcast_in_dim.11.bout_ref
  1.3 1.7 copy.9
  3.0 213.1 %shard_map.64 = bf16[4,128,768]{2,1,0:T(8,128)(2,1)} custom-call(bf16[4,128,768]{2,1,0:T(8,128)(2,1)} %lat_ref.1, bf16[1536,3072]{1,0:T(8,128)(2,1)} %bitcast.8, f32[1,3072]{1,0:T(1,128)} %bin_ref.1, bf16[3072,1536]{1,0:T(8,128)(2,1)} %bitcast.9, f32[8,768]{1,0:T(8,128)} %broadcast_in_dim.11.bout_ref, f32[4,3,3072]{2,1,0:T(4,128)} %bitcast.7), custom_call_target="tpu_custom_call" | custom-call | flops 19327352832 | bytes 18874368 | tf_op jit(solution)/shard_map/pallas_call | solution.py:415
  216.1 2.1 copy.11
